TPU v7x, 256 devices: a whole 4x4x8 slice. The times are simulated.
256 devices in a mesh: cores: 2 (over core), row: 16 (over y, x), vec: 8 (over z).
Axes of the slice: x: 4, y: 4, z: 8, core: 2. Of those that a mesh axis runs over, the one named last changes fastest.
Arguments:
- train_cores: float32 [8, 512, 256, 256], P('vec', 'cores', 'row'), may hold values from -0.01953125 to 0.01953125
- sketch: float32 [512, 128], P('cores'), may hold values from -6 to 6
- exit_sketch: float32 [256, 128], replicated, may hold values from -6 to 6
Outputs:
- rounded: float32 [8, 256, 256, 128], P('vec', 'cores', 'row')
- interface_bases: float32 [8, 512, 128], P('vec', 'cores')
- margins: float32 [8, 256, 1024], P('vec', 'cores')
All inputs are finite; a program needn't handle non-finite values.
Results may differ from a plain program's by a relative error of at most 0.0003.
Values sent between devices are 32-bit elements; how exact they have to be, the bound alone decides.
A program may use at most 128 MiB of HBM per device.

v0:
```python
import math
import jax
import jax.numpy as jnp
from jax import lax
from jax.sharding import PartitionSpec as P

MODE = 256


def broadcast(block, axis, holder):
    block = jnp.where(lax.axis_index(axis) == holder, block, jnp.zeros_like(block))
    return lax.psum(block, axis)


def product(left_mat, right_mat):
    return jnp.dot(
        left_mat, right_mat, precision=lax.Precision.HIGHEST, preferred_element_type=jnp.float32
    )


def orthonormal(gram_matrix, sketch):
    powered = product(gram_matrix, product(gram_matrix, sketch))
    chol_low = jnp.linalg.cholesky(product(powered.T, powered))
    return jax.scipy.linalg.solve_triangular(chol_low, powered.T, lower=True).T


def local(train_cores, sketch, exit_sketch):
    block_core = train_cores[0]
    full_rank = block_core.shape[0]
    mode_count = block_core.shape[1]
    kept_rank = sketch.shape[1]
    chain_len = lax.axis_size("cores")
    position = lax.axis_index("cores")
    vector_count = lax.axis_size("vec")
    identity = jnp.eye(full_rank, dtype=jnp.float32)
    zero_square = jnp.zeros((full_rank, full_rank), jnp.float32)
    row_major = block_core.reshape(full_rank * mode_count, full_rank)
    wide_core = block_core.reshape(full_rank, mode_count * full_rank)

    def forward_gram(lower_in):
        absorbed = product(lower_in.T, wide_core).reshape(full_rank * mode_count, full_rank)
        return product(absorbed.T, absorbed)

    def zero_gram(operand):
        return zero_square

    lower_prev = identity
    lower_own = identity
    gram_own = identity
    for link_index in range(chain_len):
        active = position == link_index
        partial_value = lax.cond(active, forward_gram, zero_gram, lower_prev)
        summed = jnp.where(active, lax.psum(partial_value, "row"), identity)
        factor = jnp.linalg.cholesky(summed)
        if link_index + 1 < chain_len:
            arrived = broadcast(factor, "cores", link_index)
            lower_prev = jnp.where(position == link_index + 1, arrived, lower_prev)
        lower_own = jnp.where(active, factor, lower_own)
        gram_own = jnp.where(active, summed, gram_own)
    is_last = position == chain_len - 1
    incoming = orthonormal(gram_own, exit_sketch)

    def right_map_of(incoming_frame):
        solved = jax.scipy.linalg.solve_triangular(lower_own, incoming_frame, lower=True, trans=1)
        return jnp.where(is_last, incoming_frame, solved)

    def backward_gram(incoming_frame):
        reduced = product(row_major, right_map_of(incoming_frame)).reshape(
            full_rank, mode_count * kept_rank
        )
        mixed_core = product(lower_prev.T, reduced)
        return product(mixed_core, mixed_core.T)

    frame_own = jnp.zeros((full_rank, kept_rank), jnp.float32)
    for link_index in range(chain_len):
        target = chain_len - 1 - link_index
        active = position == target
        partial_value = lax.cond(active, backward_gram, zero_gram, incoming)
        summed = jnp.where(active, lax.psum(partial_value, "row"), identity)
        frame = orthonormal(summed, sketch)
        if target > 0:
            arrived = broadcast(frame, "cores", target)
            incoming = jnp.where(position == target - 1, arrived, incoming)
        frame_own = jnp.where(active, frame, frame_own)
    reduced = product(row_major, right_map_of(incoming)).reshape(full_rank, mode_count * kept_rank)
    front_map = product(frame_own.T, lower_prev.T)
    shaped = product(front_map, reduced)
    rounded = (shaped * math.sqrt(kept_rank * MODE)).reshape(1, kept_rank, mode_count, kept_rank)
    bases_out = (frame_own * math.sqrt(full_rank))[None]
    gathered, frames_all = (
        lax.all_gather(shaped[None], "vec", axis=0, tiled=True),
        lax.all_gather(frame_own[None], "vec", axis=0, tiled=True),
    )
    start_env = jnp.einsum("az,qay->qzy", frame_own, frames_all, precision=lax.Precision.HIGHEST)
    mine_rows = shaped.reshape(kept_rank * mode_count, kept_rank)
    zero_env = jnp.zeros((vector_count, kept_rank, kept_rank), jnp.float32)

    def margin_terms(env_in):
        carried = jnp.einsum("qzw,qwx->qzx", env_in, gathered, precision=lax.Precision.HIGHEST)
        carried = carried.reshape(vector_count, kept_rank * mode_count, kept_rank)
        return jnp.einsum("cb,qcy->qby", mine_rows, carried, precision=lax.Precision.HIGHEST)

    def zero_margin(operand):
        return zero_env

    env_in = start_env
    env_own = zero_env
    for link_index in range(chain_len):
        active = position == link_index
        partial_value = lax.cond(active, margin_terms, zero_margin, env_in)
        summed = lax.psum(partial_value, "row")
        if link_index + 1 < chain_len:
            arrived = broadcast(summed, "cores", link_index)
            env_in = jnp.where(position == link_index + 1, arrived, env_in)
        env_own = jnp.where(active, summed, env_own)
    margins = env_own.transpose(1, 0, 2).reshape(kept_rank, vector_count * kept_rank)[None]
    return (rounded, bases_out, margins)


def solution(mesh):
    return jax.shard_map(
        local,
        mesh=mesh,
        in_specs=(P("vec", "cores", "row", None), P("cores", None), P()),
        out_specs=(
            P("vec", "cores", "row", None),
            P("vec", "cores", None),
            P("vec", "cores", None),
        ),
        check_vma=False,
    )
```

profile of v0, /device:TPU:1, one launch (start us, length us, event | category | flops | bytes accessed | tf_op | source)
XLA Modules:
  0.0 1188.9 jit_solution(5875113720510303117)
XLA Ops:
  7.3 7.9 copy.89
  16.3 119.6 %all-reduce.11.cloned.1.call-done = f32[256,256]{0,1:T(8,128)} async-done(((f32[256,256]{0,1:T(8,128)}), f32[256,256]{0,1:T(8,128)}) %all-reduce.11.cloned.1.call-update) | async-done | bytes 262160 | tf_op jit(solution)/shard_map/psum | solution.py:53
  136.2 11.7 cholesky.187
  148.0 9.8 custom-call.23
  158.4 11.7 cholesky.204
  173.1 32.5 %all-reduce.13.cloned.1.call-done = f32[256,256]{0,1:T(8,128)} async-done(((f32[256,256]{0,1:T(8,128)}), f32[256,256]{0,1:T(8,128)}) %all-reduce.13.cloned.1.call-update) | async-done | bytes 262160 | tf_op jit(solution)/shard_map/psum | solution.py:12
  206.6 23.0 %conditional.7 = (f32[256,256]{1,0:T(8,128)S(1)}) conditional(s32[]{:T(128)} %convert_element_type.28, () %tuple.49, (f32[256,256]{0,1:T(8,128)S(1)}, f32[256,4096]{1,0:T(8,128)}) %tuple.170), branch_computations={%region_8.10_spmd, %region_9.11_spmd} | conditional | flops 6442450944 | bytes 21495816 | solution.py:52
  206.6 8.2 fusion.96
  214.8 4.9 reshape.48
  219.6 9.9 fusion.97
  230.7 93.4 %all-reduce.15.cloned.1.call-done = f32[256,256]{0,1:T(8,128)} async-done(((f32[256,256]{0,1:T(8,128)}), f32[256,256]{0,1:T(8,128)}) %all-reduce.15.cloned.1.call-update) | async-done | bytes 262160 | tf_op jit(solution)/shard_map/psum | solution.py:53
  326.2 11.7 cholesky.221
  338.1 9.8 custom-call.24
  348.5 11.7 cholesky.238
  360.4 1.6 fusion.51
  364.0 12.1 %cholesky.253 = f32[128,128]{1,0:T(8,128)S(1)} custom-call(f32[128,128]{1,0:T(8,128)S(1)} %fusion.69), custom_call_target="Cholesky" | custom-call | tf_op jit(solution)/shard_map/jit(cholesky)/cholesky | solution.py:23
  377.4 9.8 custom-call.25
  390.3 42.7 %conditional.8 = (f32[256,256]{1,0:T(8,128)S(1)}) conditional(s32[]{:T(128)} %convert_element_type.28, () %tuple.53, (pred[]{:T(512)}, f32[256,256]{0,1:T(8,128)S(1)}, f32[256,128]{0,1:T(8,128)S(1)}, f32[4096,256]{1,0:T(8,128)}, f32[256,256]{0,1:T(8,128)S(1)}) %tuple.167), branch_computations={%region_13.17_spmd, %region_14.19_spmd} | conditional | flops 4907548672 | bytes 23855310 | solution.py:78
  390.8 3.8 while.6
  394.6 19.7 %custom-call.21 = f32[2,128,128]{1,2,0:T(8,128)S(1)} custom-call(f32[2,128,128]{2,1,0:T(8,128)S(1)} %get-tuple-element.113), custom_call_target="InvertDiagBlocksLowerTriangular" | custom-call | tf_op jit(solution)/shard_map/cond/branch_1_fun/jit(_solve_triangular)/triangular_solve | solution.py:64
  415.0 6.7 convolution_bitcast_fusion.2
  421.7 1.9 copy.42
  423.6 1.9 reshape.49
  425.5 3.6 fusion.99
  429.1 3.6 fusion.100
  433.9 91.5 %all-reduce.17.cloned.1.call-done = f32[256,256]{0,1:T(8,128)} async-done(((f32[256,256]{0,1:T(8,128)}), f32[256,256]{0,1:T(8,128)}) %all-reduce.17.cloned.1.call-update) | async-done | bytes 262160 | tf_op jit(solution)/shard_map/psum | solution.py:79
  529.0 11.7 cholesky.264
  542.1 9.8 custom-call.26
  552.9 28.4 %all-reduce.19.cloned.1.call-done = f32[256,128]{0,1:T(8,128)} async-done(((f32[256,128]{0,1:T(8,128)}), f32[256,128]{0,1:T(8,128)}) %all-reduce.19.cloned.1.call-update) | async-done | bytes 131088 | tf_op jit(solution)/shard_map/psum | solution.py:12
  581.3 6.4 conditional.9
  588.6 131.1 %all-reduce.21.cloned.1.call-done = f32[256,256]{0,1:T(8,128)} async-done(((f32[256,256]{0,1:T(8,128)}), f32[256,256]{0,1:T(8,128)}) %all-reduce.21.cloned.1.call-update) | async-done | bytes 262160 | tf_op jit(solution)/shard_map/psum | solution.py:79
  721.5 11.7 cholesky.275
  734.5 9.8 custom-call.27
  745.7 4.0 while.8
  749.7 19.7 %custom-call.28 = f32[2,128,128]{1,2,0:T(8,128)S(1)} custom-call(f32[2,128,128]{2,1,0:T(8,128)S(1)} %get-tuple-element.115), custom_call_target="InvertDiagBlocksLowerTriangular" | custom-call | tf_op jit(solution)/shard_map/jit(_solve_triangular)/triangular_solve | solution.py:64
  770.3 6.5 convolution_bitcast_fusion.4
  776.8 1.9 copy.69
  778.7 1.7 reshape.56
  780.7 2.2 fusion.107
  784.4 2.2 convolution_bitcast_fusion.5
  786.7 95.5 %all-gather.7.cloned.1.call-done = f32[1024,2048]{1,0:T(8,128)} async-done(((f32[128,2048]{1,0:T(8,128)}), f32[1024,2048]{1,0:T(8,128)}) %all-gather.7.cloned.1.call-update) | async-done | bytes 8388624 | tf_op jit(solution)/shard_map/all_gather | solution.py:91
  883.5 129.1 %all-reduce.23.cloned.1.call-done = f32[8,128,128]{1,2,0:T(8,128)} async-done(((f32[8,128,128]{1,2,0:T(8,128)}), f32[8,128,128]{1,2,0:T(8,128)}) %all-reduce.23.cloned.1.call-update) | async-done | bytes 524304 | tf_op jit(solution)/shard_map/psum | solution.py:111
  1013.5 33.1 %all-reduce.25.cloned.1.call-done = f32[8,128,128]{1,2,0:T(8,128)} async-done(((f32[8,128,128]{1,2,0:T(8,128)}), f32[8,128,128]{1,2,0:T(8,128)}) %all-reduce.25.cloned.1.call-update) | async-done | bytes 524304 | tf_op jit(solution)/shard_map/psum | solution.py:12
  1046.6 38.8 %conditional.11 = (f32[8,128,128]{1,2,0:T(8,128)}) conditional(s32[]{:T(128)} %convert_element_type.28, () %tuple.56, (pred[]{:T(512)}, f32[8,128,128]{1,2,0:T(8,128)}, f32[8,128,128]{1,2,0:T(8,128)S(1)}, f32[8,128,2048]{2,1,0:T(8,128)}, f32[2048,128]{1,0:T(8,128)S(1)}) %tuple.172), branch_computations={%region_24.29_spmd, %region_25.30_spmd} | conditional | flops 6442582016 | bytes 46661640 | solution.py:110
  1048.2 11.7 fusion.2
  1059.9 9.3 reshape.52
  1069.2 16.2 %convolution_bitcast_fusion.1 = f32[8,128,128]{1,2,0:T(8,128)} fusion(f32[8,2048,128]{2,1,0:T(8,128)} %reshape.52, f32[2048,128]{1,0:T(8,128)S(1)} %get-tuple-element.89), kind=kOutput, calls=%fused_computation.2 | convolution fusion | flops 3221225472 | bytes 9961472 | tf_op jit(solution)/shard_map/cond/branch_1_fun/cb,qcy->qby/dot_general | solution.py:101
  1087.4 92.6 %all-reduce.27.cloned.1.call-done = f32[8,128,128]{1,2,0:T(8,128)} async-done(((f32[8,128,128]{1,2,0:T(8,128)}), f32[8,128,128]{1,2,0:T(8,128)}) %all-reduce.27.cloned.1.call-update) | async-done | bytes 524304 | tf_op jit(solution)/shard_map/psum | solution.py:111
  (155 shorter events, 45.1 us)
Async XLA Ops:
  7.2 518.2 %copy-start = (f32[256,128]{1,0:T(8,128)S(1)}, f32[256,128]{1,0:T(8,128)}, u32[]{:S(2)}) copy-start(f32[256,128]{1,0:T(8,128)} %param.22) | copy-start | bytes 393220
  7.2 128.7 %all-reduce.11.cloned.1.call-start = ((), (), s32[]{:S(2)}) async-start(), calls=%async_computation | async-start | bytes 524288 | tf_op jit(solution)/shard_map/psum | solution.py:53
  16.1 189.5 %all-reduce.13.cloned.1.call-start = ((), (), s32[]{:S(2)}) async-start(), calls=%async_computation.1 | async-start | bytes 524288 | tf_op jit(solution)/shard_map/psum | solution.py:12
  173.0 151.1 %all-reduce.15.cloned.1.call-start = ((), (), s32[]{:S(2)}) async-start(), calls=%async_computation.2 | async-start | bytes 524288 | tf_op jit(solution)/shard_map/psum | solution.py:53
  206.5 153.8 %copy-start.3 = (f32[256,256]{0,1:T(8,128)S(1)}, f32[256,256]{0,1:T(8,128)}, u32[]{:S(2)}) copy-start(f32[256,256]{0,1:T(8,128)} %all-reduce.11.cloned.1.call-done) | copy-start | bytes 786436
  206.6 153.8 %copy-start.8 = (f32[256,128]{1,0:T(8,128)S(1)}, f32[256,128]{1,0:T(8,128)}, u32[]{:S(2)}) copy-start(f32[256,128]{1,0:T(8,128)} %param.23) | copy-start | bytes 393220
  230.4 295.0 %all-reduce.17.cloned.1.call-start = ((), (), s32[]{:S(2)}) async-start(), calls=%async_computation.3 | async-start | bytes 524288 | tf_op jit(solution)/shard_map/psum | solution.py:79
  433.8 147.4 %all-reduce.19.cloned.1.call-start = ((), (), s32[]{:S(2)}) async-start(), calls=%async_computation.4 | async-start | bytes 262144 | tf_op jit(solution)/shard_map/psum | solution.py:12
  552.9 166.9 %all-reduce.21.cloned.1.call-start = ((), (), s32[]{:S(2)}) async-start(), calls=%async_computation.5 | async-start | bytes 524288 | tf_op jit(solution)/shard_map/psum | solution.py:79
  581.3 163.0 %copy-start.7 = (f32[256,128]{0,1:T(8,128)S(1)}, f32[256,128]{0,1:T(8,128)}, u32[]{:S(2)}) copy-start(f32[256,128]{0,1:T(8,128)} %fusion.24) | copy-start | bytes 393220
  588.6 195.9 %all-gather.5.cloned.1.call-start = ((), (), s32[]{:S(2)}) async-start(), calls=%async_computation.9 | async-start | bytes 1179648 | tf_op jit(solution)/shard_map/all_gather | solution.py:92
  745.3 136.8 %all-gather.7.cloned.1.call-start = ((), (), s32[]{:S(2)}) async-start(), calls=%async_computation.10 | async-start | bytes 9437184 | tf_op jit(solution)/shard_map/all_gather | solution.py:91
  776.8 3.6 copy-start.4
  783.0 229.6 %all-reduce.23.cloned.1.call-start = ((), (), s32[]{:S(2)}) async-start(), calls=%async_computation.6 | async-start | bytes 1048576 | tf_op jit(solution)/shard_map/psum | solution.py:111
  882.6 0.8 copy-start.5
  883.4 163.2 %all-reduce.25.cloned.1.call-start = ((), (), s32[]{:S(2)}) async-start(), calls=%async_computation.7 | async-start | bytes 1048576 | tf_op jit(solution)/shard_map/psum | solution.py:12
  1013.4 166.6 %all-reduce.27.cloned.1.call-start = ((), (), s32[]{:S(2)}) async-start(), calls=%async_computation.8 | async-start | bytes 1048576 | tf_op jit(solution)/shard_map/psum | solution.py:111
  1046.6 39.6 %copy-start.2 = (f32[128,2048]{1,0:T(8,128)S(1)}, f32[128,2048]{1,0:T(8,128)}, u32[]{:S(2)}) copy-start(f32[128,2048]{1,0:T(8,128)} %fusion.107) | copy-start | bytes 3145732
  1085.4 94.7 %copy-start.6 = (f32[8,128,128]{1,2,0:T(8,128)S(1)}, f32[8,128,128]{1,2,0:T(8,128)}, u32[]{:S(2)}) copy-start(f32[8,128,128]{1,2,0:T(8,128)} %all-reduce.23.cloned.1.call-done) | copy-start | bytes 1572868
  1085.4 96.8 %copy-start.1 = (f32[256,128]{1,0:T(8,128)S(1)}, f32[256,128]{1,0:T(8,128)}, u32[]{:S(2)}) copy-start(f32[256,128]{1,0:T(8,128)} %param.22) | copy-start | bytes 393220
Sparse Core Ops, SparseCore 0:
  16.2 119.6 all-reduce.10
  173.2 32.3 all-reduce.12
  230.5 93.5 all-reduce.14
  434.0 91.3 all-reduce.16
  553.0 28.2 all-reduce.18
  588.7 131.0 all-reduce.20
  745.5 37.0 all-gather.4
  785.1 96.9 all-gather.6
  886.2 126.2 all-reduce.22
  1015.6 30.9 all-reduce.24
  1085.5 94.4 all-reduce.26
where the time goes:
time: 1200 us; the launch traced here: 1190 us
  waiting for transfers between devices  847 us (71%)
  other arithmetic  183 us (15%)
  matrix products  84.3 us (7%)
  local copies, waits for them, and re-layouts  48.8 us (4%)
  between operations  17.2 us (1%)
    psum x4, waiting for transfers between devices, local(): summed = jnp.where(active, lax.psum(partial_value, 'row'), identity)  436 us
    psum x2, waiting for transfers between devices, local(): summed = lax.psum(partial_value, 'row')  222 us
    all_gather x1, waiting for transfers between devices, local(): lax.all_gather(shaped[None], 'vec', axis=0, tiled=True)  95.5 us
    psum x3, waiting for transfers between devices, broadcast(): return lax.psum(block, axis)  94 us
    another operation x13, other arithmetic, local(): factor = jnp.linalg.cholesky(summed)  68.5 us
    dot_general x17, matrix products, product(): jnp.dot(left_mat, right_mat, precision=lax.Precision.HIGHEST, preferred_e...  49.5 us
    another operation x8, other arithmetic, right_map_of(): jax.scipy.linalg.solve_triangular(lower_own, incoming_frame, lower=True,...  39.4 us
    another operation x9, other arithmetic, orthonormal(): chol_low = jnp.linalg.cholesky(product(powered.T, powered))  37.6 us
  transfers between devices with their start and end apart: 11, of which 10 were waited for; matrix products, arithmetic and copies ran while one was open for 4% of the time, Pallas kernels for 0%

commit v1 on v0

--- a/solution.py
+++ b/solution.py
@@ -88,7 +88,9 @@
     rounded = (shaped * math.sqrt(kept_rank * MODE)).reshape(1, kept_rank, mode_count, kept_rank)
     bases_out = (frame_own * math.sqrt(full_rank))[None]
     gathered, frames_all = (
-        lax.all_gather(shaped[None], "vec", axis=0, tiled=True),
+        jnp.concatenate(
+            lax.all_to_all(jnp.stack([shaped[None]] * lax.axis_size("vec")), "vec", 0, 0), axis=0
+        ),
         lax.all_gather(frame_own[None], "vec", axis=0, tiled=True),
     )
     start_env = jnp.einsum("az,qay->qzy", frame_own, frames_all, precision=lax.Precision.HIGHEST)

time: 1200 us -> 1270 us (1.058)
  waiting for transfers between devices: 847 us -> 885 us
  local copies, waits for them, and re-layouts: 48.8 us -> 68.2 us
  starting transfers between devices: 1.05 us -> 16.1 us
    all_to_all x0 -> x1, waiting for transfers between devices: none -> 120 us  [local(): lax.all_to_all(jnp.stack([shaped[None]] * lax.axis_size('vec')), 'vec', 0...]
    all_gather x1 -> x0, waiting for transfers between devices: 95.5 us -> none  [local(): lax.all_gather(shaped[None], 'vec', axis=0, tiled=True)]
    all_gather x1, waiting for transfers between devices: 0.02 us -> 63.2 us  [local(): lax.all_gather(frame_own[None], 'vec', axis=0, tiled=True)]
    psum x4, waiting for transfers between devices: 436 us -> 404 us  [local(): summed = jnp.where(active, lax.psum(partial_value, 'row'), identity)]
    psum x3, waiting for transfers between devices: 94 us -> 70.5 us  [broadcast(): return lax.psum(block, axis)]
    dot_general x5, local copies, waits for them, and re-layouts: 4.01 us -> 19.4 us  [product(): jnp.dot(left_mat, right_mat, precision=lax.Precision.HIGHEST, preferred_e...]
  transfers between devices with their start and end apart: 11 -> 11, of which waited for: 10 -> 11; matrix products, arithmetic and copies ran while one was open for 4% -> 4% of each run, Pallas kernels for 0% -> 0%
where the time goes in v1:
time: 1270 us; the launch traced here: 1260 us
  waiting for transfers between devices  885 us (70%)
  other arithmetic  183 us (14%)
  matrix products  84.1 us (7%)
  local copies, waits for them, and re-layouts  68.2 us (5%)
  between operations  17.7 us (1%)
  starting transfers between devices  16.1 us (1%)
    psum x4, waiting for transfers between devices, local(): summed = jnp.where(active, lax.psum(partial_value, 'row'), identity)  404 us
    psum x2, waiting for transfers between devices, local(): summed = lax.psum(partial_value, 'row')  226 us
    all_to_all x1, waiting for transfers between devices, local(): lax.all_to_all(jnp.stack([shaped[None]] * lax.axis_size('vec')), 'vec', 0...  120 us
    psum x3, waiting for transfers between devices, broadcast(): return lax.psum(block, axis)  70.5 us
    another operation x13, other arithmetic, local(): factor = jnp.linalg.cholesky(summed)  68.5 us
    all_gather x1, waiting for transfers between devices, local(): lax.all_gather(frame_own[None], 'vec', axis=0, tiled=True)  63.2 us
    dot_general x17, matrix products, product(): jnp.dot(left_mat, right_mat, precision=lax.Precision.HIGHEST, preferred_e...  48.5 us
    another operation x8, other arithmetic, right_map_of(): jax.scipy.linalg.solve_triangular(lower_own, incoming_frame, lower=True,...  39.4 us
  transfers between devices with their start and end apart: 11, of which 11 were waited for; matrix products, arithmetic and copies ran while one was open for 4% of the time, Pallas kernels for 0%

profile of v1, /device:TPU:1, one launch (start us, length us, event | category | flops | bytes accessed | tf_op | source)
XLA Modules:
  0.0 1258.4 jit_solution(15472358871664324414)
XLA Ops:
  7.3 7.9 copy.130
  16.4 119.5 %all-reduce.11.cloned.1.call-done = f32[256,256]{0,1:T(8,128)} async-done(((f32[256,256]{0,1:T(8,128)}), f32[256,256]{0,1:T(8,128)}) %all-reduce.11.cloned.1.call-update) | async-done | bytes 262160 | tf_op jit(solution)/shard_map/psum | solution.py:53
  136.2 11.7 cholesky.187
  148.0 9.8 custom-call.23
  158.4 11.7 cholesky.204
  173.1 32.5 %all-reduce.13.cloned.1.call-done = f32[256,256]{0,1:T(8,128)} async-done(((f32[256,256]{0,1:T(8,128)}), f32[256,256]{0,1:T(8,128)}) %all-reduce.13.cloned.1.call-update) | async-done | bytes 262160 | tf_op jit(solution)/shard_map/psum | solution.py:12
  206.6 23.0 %conditional.7 = (f32[256,256]{1,0:T(8,128)S(1)}) conditional(s32[]{:T(128)} %convert_element_type.28, () %tuple.49, (f32[256,256]{0,1:T(8,128)S(1)}, f32[256,4096]{1,0:T(8,128)}) %tuple.176), branch_computations={%region_8.10_spmd, %region_9.11_spmd} | conditional | flops 6442450944 | bytes 21495816 | solution.py:52
  206.6 8.2 fusion.96
  214.8 4.9 reshape.52
  219.6 9.9 fusion.97
  230.4 8.8 all-reduce.17.cloned.1.call-start
  239.2 84.9 %all-reduce.15.cloned.1.call-done = f32[256,256]{0,1:T(8,128)} async-done(((f32[256,256]{0,1:T(8,128)}), f32[256,256]{0,1:T(8,128)}) %all-reduce.15.cloned.1.call-update) | async-done | bytes 262160 | tf_op jit(solution)/shard_map/psum | solution.py:53
  326.3 11.7 cholesky.221
  338.1 9.8 custom-call.24
  348.5 11.7 cholesky.238
  364.0 11.9 cholesky.253
  377.3 9.8 custom-call.25
  390.1 43.3 %conditional.8 = (f32[256,256]{1,0:T(8,128)S(1)}) conditional(s32[]{:T(128)} %convert_element_type.28, () %tuple.53, (pred[]{:T(512)}, f32[256,256]{0,1:T(8,128)S(1)}, f32[256,128]{0,1:T(8,128)S(1)}, f32[4096,256]{1,0:T(8,128)}, f32[256,256]{0,1:T(8,128)S(1)}) %tuple.173), branch_computations={%region_13.17_spmd, %region_14.19_spmd} | conditional | flops 4907548672 | bytes 23855310 | solution.py:78
  390.7 3.8 while.6
  394.6 19.7 %custom-call.21 = f32[2,128,128]{1,2,0:T(8,128)S(1)} custom-call(f32[2,128,128]{2,1,0:T(8,128)S(1)} %get-tuple-element.113), custom_call_target="InvertDiagBlocksLowerTriangular" | custom-call | tf_op jit(solution)/shard_map/cond/branch_1_fun/jit(_solve_triangular)/triangular_solve | solution.py:64
  415.0 6.7 convolution_bitcast_fusion.2
  423.5 2.2 reshape.53
  425.7 3.6 fusion.99
  429.2 3.6 fusion.100
  434.4 91.5 %all-reduce.17.cloned.1.call-done = f32[256,256]{0,1:T(8,128)} async-done(((f32[256,256]{0,1:T(8,128)}), f32[256,256]{0,1:T(8,128)}) %all-reduce.17.cloned.1.call-update) | async-done | bytes 262160 | tf_op jit(solution)/shard_map/psum | solution.py:79
  529.5 11.7 cholesky.264
  542.6 9.8 custom-call.26
  553.5 4.0 while.8
  557.5 19.7 %custom-call.28 = f32[2,128,128]{1,2,0:T(8,128)S(1)} custom-call(f32[2,128,128]{2,1,0:T(8,128)S(1)} %get-tuple-element.115), custom_call_target="InvertDiagBlocksLowerTriangular" | custom-call | tf_op jit(solution)/shard_map/jit(_solve_triangular)/triangular_solve | solution.py:64
  577.2 4.7 all-reduce.19.cloned.1.call-done
  583.9 3.4 conditional.9
  589.3 6.5 convolution_bitcast_fusion.4
  595.8 17.2 %copy.108 = f32[4096,128]{1,0:T(8,128)} copy(f32[4096,128]{0,1:T(8,128)S(1)} %convolution_bitcast_fusion.4) | data formatting | bytes 4194304 | tf_op jit(solution)/shard_map/dot_general | solution.py:16
  614.8 107.5 %all-reduce.21.cloned.1.call-done = f32[256,256]{0,1:T(8,128)} async-done(((f32[256,256]{0,1:T(8,128)}), f32[256,256]{0,1:T(8,128)}) %all-reduce.21.cloned.1.call-update) | async-done | bytes 262160 | tf_op jit(solution)/shard_map/psum | solution.py:79
  724.0 11.7 cholesky.275
  737.1 9.8 custom-call.27
  748.8 4.3 stack.3
  753.1 6.7 all-to-all-start
  760.8 63.2 %all-gather.3.cloned.1.call-done = f32[2048,128]{0,1:T(8,128)} async-done(((f32[256,128]{0,1:T(8,128)}), f32[2048,128]{0,1:T(8,128)}) %all-gather.3.cloned.1.call-update) | async-done | bytes 1048592 | tf_op jit(solution)/shard_map/all_gather | solution.py:94
  824.0 2.2 convolution_bitcast_fusion.5
  826.2 120.4 %all-to-all-done = f32[8,1,128,2048]{3,2,1,0:T(8,128)} async-done(((f32[8,1,128,2048]{3,2,1,0:T(8,128)}), f32[8,1,128,2048]{3,2,1,0:T(8,128)}, u32[]{:S(2)}, u32[]{:S(2)}) %all-to-all-start) | async-done | bytes 8388640 | tf_op jit(solution)/shard_map/all_to_all | solution.py:92
  947.7 133.9 %all-reduce.23.cloned.1.call-done = f32[8,128,128]{1,2,0:T(8,128)} async-done(((f32[8,128,128]{1,2,0:T(8,128)}), f32[8,128,128]{1,2,0:T(8,128)}) %all-reduce.23.cloned.1.call-update) | async-done | bytes 524304 | tf_op jit(solution)/shard_map/psum | solution.py:113
  1082.5 33.3 %all-reduce.25.cloned.1.call-done = f32[8,128,128]{1,2,0:T(8,128)} async-done(((f32[8,128,128]{1,2,0:T(8,128)}), f32[8,128,128]{1,2,0:T(8,128)}) %all-reduce.25.cloned.1.call-update) | async-done | bytes 524304 | tf_op jit(solution)/shard_map/psum | solution.py:12
  1115.8 38.6 %conditional.11 = (f32[8,128,128]{1,2,0:T(8,128)}) conditional(s32[]{:T(128)} %convert_element_type.28, () %tuple.56, (pred[]{:T(512)}, f32[8,128,128]{1,2,0:T(8,128)}, f32[8,128,128]{1,2,0:T(8,128)S(1)}, f32[8,128,2048]{2,1,0:T(8,128)}, f32[2048,128]{1,0:T(8,128)S(1)}) %tuple.59), branch_computations={%region_24.29_spmd, %region_25.30_spmd} | conditional | flops 6442582016 | bytes 46661640 | solution.py:112
  1117.2 11.7 fusion.2
  1128.9 9.3 reshape.56
  1138.2 16.2 %convolution_bitcast_fusion.1 = f32[8,128,128]{1,2,0:T(8,128)} fusion(f32[8,2048,128]{2,1,0:T(8,128)} %reshape.56, f32[2048,128]{1,0:T(8,128)S(1)} %get-tuple-element.89), kind=kOutput, calls=%fused_computation.2 | convolution fusion | flops 3221225472 | bytes 9961472 | tf_op jit(solution)/shard_map/cond/branch_1_fun/cb,qcy->qby/dot_general | solution.py:103
  1156.4 92.6 %all-reduce.27.cloned.1.call-done = f32[8,128,128]{1,2,0:T(8,128)} async-done(((f32[8,128,128]{1,2,0:T(8,128)}), f32[8,128,128]{1,2,0:T(8,128)}) %all-reduce.27.cloned.1.call-update) | async-done | bytes 524304 | tf_op jit(solution)/shard_map/psum | solution.py:113
  (157 shorter events, 51.8 us)
Async XLA Ops:
  7.2 518.7 %copy-start = (f32[256,128]{1,0:T(8,128)S(1)}, f32[256,128]{1,0:T(8,128)}, u32[]{:S(2)}) copy-start(f32[256,128]{1,0:T(8,128)} %param.22) | copy-start | bytes 393220
  7.2 128.7 %all-reduce.11.cloned.1.call-start = ((), (), s32[]{:S(2)}) async-start(), calls=%async_computation.1 | async-start | bytes 524288 | tf_op jit(solution)/shard_map/psum | solution.py:53
  16.1 189.5 %all-reduce.13.cloned.1.call-start = ((), (), s32[]{:S(2)}) async-start(), calls=%async_computation.2 | async-start | bytes 524288 | tf_op jit(solution)/shard_map/psum | solution.py:12
  173.0 151.1 %all-reduce.15.cloned.1.call-start = ((), (), s32[]{:S(2)}) async-start(), calls=%async_computation.3 | async-start | bytes 524288 | tf_op jit(solution)/shard_map/psum | solution.py:53
  206.5 153.8 %copy-start.2 = (f32[256,256]{0,1:T(8,128)S(1)}, f32[256,256]{0,1:T(8,128)}, u32[]{:S(2)}) copy-start(f32[256,256]{0,1:T(8,128)} %all-reduce.11.cloned.1.call-done) | copy-start | bytes 786436
  206.5 153.8 %copy-start.9 = (f32[256,128]{1,0:T(8,128)S(1)}, f32[256,128]{1,0:T(8,128)}, u32[]{:S(2)}) copy-start(f32[256,128]{1,0:T(8,128)} %param.23) | copy-start | bytes 393220
  230.4 295.5 %all-reduce.17.cloned.1.call-start = ((), (), s32[]{:S(2)}) async-start(), calls=%async_computation.4 | async-start | bytes 524288 | tf_op jit(solution)/shard_map/psum | solution.py:79
  434.3 147.6 %all-reduce.19.cloned.1.call-start = ((), (), s32[]{:S(2)}) async-start(), calls=%async_computation.5 | async-start | bytes 262144 | tf_op jit(solution)/shard_map/psum | solution.py:12
  553.4 168.9 %all-reduce.21.cloned.1.call-start = ((), (), s32[]{:S(2)}) async-start(), calls=%async_computation.6 | async-start | bytes 524288 | tf_op jit(solution)/shard_map/psum | solution.py:79
  577.2 6.6 copy-start.8
  613.0 133.9 %copy-start.7 = (f32[256,128]{0,1:T(8,128)S(1)}, f32[256,128]{0,1:T(8,128)}, u32[]{:S(2)}) copy-start(f32[256,128]{0,1:T(8,128)} %fusion.24) | copy-start | bytes 393220
  747.2 5.9 copy-start.3
  753.1 193.5 %all-to-all-start = ((f32[8,1,128,2048]{3,2,1,0:T(8,128)}), f32[8,1,128,2048]{3,2,1,0:T(8,128)}, u32[]{:S(2)}, u32[]{:S(2)}) async-start(f32[8,1,128,2048]{3,2,1,0:T(8,128)} %stack.3), calls=%async_computation | async-start | bytes 16777216 | tf_op jit(solution)/shard_map/all_to_all | solution.py:92
  759.8 64.1 %all-gather.3.cloned.1.call-start = ((), (), s32[]{:S(2)}) async-start(), calls=%async_computation.10 | async-start | bytes 1179648 | tf_op jit(solution)/shard_map/all_gather | solution.py:94
  760.6 321.0 %all-reduce.23.cloned.1.call-start = ((), (), s32[]{:S(2)}) async-start(), calls=%async_computation.7 | async-start | bytes 1048576 | tf_op jit(solution)/shard_map/psum | solution.py:113
  946.8 0.8 copy-start.5
  947.6 168.1 %all-reduce.25.cloned.1.call-start = ((), (), s32[]{:S(2)}) async-start(), calls=%async_computation.8 | async-start | bytes 1048576 | tf_op jit(solution)/shard_map/psum | solution.py:12
  1082.4 166.6 %all-reduce.27.cloned.1.call-start = ((), (), s32[]{:S(2)}) async-start(), calls=%async_computation.9 | async-start | bytes 1048576 | tf_op jit(solution)/shard_map/psum | solution.py:113
  1115.8 38.6 %copy-start.4 = (f32[256,128]{0,1:T(8,128)S(1)}, f32[256,128]{0,1:T(8,128)}, u32[]{:S(2)}) copy-start(f32[256,128]{0,1:T(8,128)} %copy-done.3) | copy-start | bytes 393220
  1154.4 94.7 %copy-start.6 = (f32[8,128,128]{1,2,0:T(8,128)S(1)}, f32[8,128,128]{1,2,0:T(8,128)}, u32[]{:S(2)}) copy-start(f32[8,128,128]{1,2,0:T(8,128)} %all-reduce.23.cloned.1.call-done) | copy-start | bytes 1572868
  1154.4 96.8 %copy-start.1 = (f32[256,128]{1,0:T(8,128)S(1)}, f32[256,128]{1,0:T(8,128)}, u32[]{:S(2)}) copy-start(f32[256,128]{1,0:T(8,128)} %param.22) | copy-start | bytes 393220
Sparse Core Ops, SparseCore 0:
  16.2 119.6 all-reduce.10
  173.1 32.3 all-reduce.12
  230.5 93.5 all-reduce.14
  434.4 91.4 all-reduce.16
  553.5 28.3 all-reduce.18
  588.2 134.0 all-reduce.20
  763.2 60.7 all-gather.2
  947.8 133.7 all-reduce.22
  1084.7 30.9 all-reduce.24
  1154.5 94.4 all-reduce.26
